TPU v7x, 32 devices: a whole 2x2x4 slice. The times are simulated.
32 devices in a mesh: group: 2 (over y), seq: 16 (over z, x, core).
Axes of the slice: x: 2, y: 2, z: 4, core: 2. Of those that a mesh axis runs over, the one named last changes fastest.
Arguments:
- node_feats: bfloat16 [16384, 1024], P(('group', 'seq')), parts along dimension 0, may hold values from -6 to 6
- struct_feats: float32 [16384, 128], P(('group', 'seq')), parts along dimension 0, may hold values from -6 to 6
- op_blocks: float32 [256, 3, 64, 64], P(('group', 'seq')), parts along dimension 0, may hold values from -0.07 to 0.07
- laplace_index: int32 [256, 3], P(('group', 'seq')), parts along dimension 0, may hold values from 0 to 127, as said below
- graph_links: int32 [256, 3], P(('group', 'seq')), parts along dimension 0, may hold values from 0 to 127, as said below
- expander_slot: int32 [256, 4], P(('group', 'seq')), parts along dimension 0, may hold values from 0 to 7
- series_coef: float32 [9], replicated, may hold values from 0.3 to 1
- encode_weight: bfloat16 [128, 1024], replicated, may hold values from -0.5 to 0.5
- qkv_weight: bfloat16 [1024, 3072], replicated, may hold values from -0.1875 to 0.1875
- out_weight: bfloat16 [1024, 1024], replicated, may hold values from -0.1875 to 0.1875
Outputs:
- mixed: bfloat16 [16384, 1024], P(('group', 'seq')), parts along dimension 0
There are 2 independent parts, one for each index of `group`. A program takes and returns all parts, laid end to end along the dimension named above; an argument that names none is the same for every part. Nothing has to cross between parts.
Inputs may be any that keep to these rules, and one draw needn't show every extreme that they name: `laplace_index`: each entry lies within 2 blocks of its row's block. `graph_links`: each entry lies within 2 blocks of its row's block.
All inputs are finite; a program needn't handle non-finite values.
Results may differ from a plain program's by a relative error of at most 0.012.
The roundings to bfloat16 on the way count: a program that leaves them out, or rounds other values in their place, can miss the bound.
Values may be sent and summed in bfloat16 or wider, within the bound.
A program may use at most 192 MiB of HBM per device.

v0:
```python
import jax
import jax.numpy as jnp
from jax import lax
from jax.sharding import PartitionSpec as P

D = 1024
HEADS = 16
HD = 64
BS = 64
DEG = 8
NEXP = 4
REACH = 2


def extended(x, sides, width):
    for axis, dim in sides:
        peers, length = (lax.axis_size(axis), x.shape[dim])
        up = [(i, (i + 1) % peers) for i in range(peers - 1)]
        down = [(j, i) for i, j in up]
        last = lax.slice_in_dim(x, length - width, length, axis=dim)
        first = lax.slice_in_dim(x, 0, width, axis=dim)
        before = lax.ppermute(last, axis, up)
        after = lax.ppermute(first, axis, down)
        x = jnp.concatenate([before, x, after], axis=dim)
    return x


def partner(value, axis, distance):
    mask = 2**distance
    pairs = [(source, source ^ mask) for source in range(lax.axis_size(axis))]
    return lax.ppermute(value, axis, pairs)


def apply_operator(field, op_blocks, laplace_index, first_block):
    count = op_blocks.shape[0]
    padded = extended(field, (("seq", 0),), REACH * BS)
    pooled = padded.reshape(count + 2 * REACH, BS, field.shape[1])
    position = laplace_index - first_block + REACH
    picked = pooled[position]
    result = jnp.einsum("bjst,bjtc->bsc", op_blocks, picked, precision=lax.Precision.HIGHEST)
    return result.reshape(field.shape)


def on_device(
    node_feats,
    struct_feats,
    op_blocks,
    laplace_index,
    graph_links,
    expander_slot,
    series_coef,
    encode_weight,
    qkv_weight,
    out_weight,
):
    count = op_blocks.shape[0]
    first_block = lax.axis_index("seq") * count
    previous = struct_feats
    current = apply_operator(previous, op_blocks, laplace_index, first_block)
    encoding = series_coef[0] * previous + series_coef[1] * current
    for degree in range(2, DEG + 1):
        following = 2.0 * apply_operator(current, op_blocks, laplace_index, first_block) - previous
        encoding = encoding + series_coef[degree] * following
        previous, current = (current, following)
    encoded = jnp.dot(
        encoding.astype(jnp.bfloat16), encode_weight, preferred_element_type=jnp.float32
    )
    blended = (node_feats.astype(jnp.float32) + encoded).astype(jnp.bfloat16)
    projected = jnp.dot(blended, qkv_weight, preferred_element_type=jnp.float32)
    queries = projected[:, :D].astype(jnp.bfloat16)
    keyvals = projected[:, D:].astype(jnp.bfloat16)
    rim_rows = REACH * BS
    near_pool = extended(keyvals, (("seq", 0),), rim_rows)
    levels = lax.axis_size("seq").bit_length() - 1
    far_parts = []
    for link in range(NEXP):
        bit_number = link * (levels - 1) // (NEXP - 1)
        far_rows = partner(keyvals, "seq", bit_number)
        far_parts.append(far_rows)
    pool_rows = jnp.concatenate([near_pool] + far_parts, axis=0)
    pool_blocks = pool_rows.reshape(-1, BS, 2 * D)
    own_slot = jnp.arange(count, dtype=jnp.int32)[:, None] + REACH
    graph_slot = graph_links - first_block + REACH
    far_base = count + 2 * REACH + jnp.arange(NEXP, dtype=jnp.int32) * count
    far_slot = far_base[None, :] + expander_slot
    key_slots = jnp.concatenate([own_slot, graph_slot, far_slot], axis=1)
    picked = pool_blocks[key_slots].reshape(count, -1, 2 * D)
    keys = picked[:, :, :D].reshape(count, -1, HEADS, HD)
    values = picked[:, :, D:].reshape(count, -1, HEADS, HD)
    qheads = queries.reshape(count, BS, HEADS, HD)
    scale = 1.0 / HD**0.5
    scores = jnp.einsum("bqhd,bkhd->bhqk", qheads, keys, preferred_element_type=jnp.float32) * scale
    weights = jax.nn.softmax(scores, axis=-1).astype(jnp.bfloat16)
    attended = jnp.einsum("bhqk,bkhd->bqhd", weights, values, preferred_element_type=jnp.float32)
    attended = attended.reshape(count * BS, D).astype(jnp.bfloat16)
    return jnp.dot(attended, out_weight, preferred_element_type=jnp.float32).astype(jnp.bfloat16)


def solution(mesh):
    placed = (
        P(("group", "seq"), None),
        P(("group", "seq"), None),
        P(("group", "seq"), None, None, None),
        P(("group", "seq"), None),
        P(("group", "seq"), None),
        P(("group", "seq"), None),
        P(),
        P(),
        P(),
        P(),
    )
    return jax.shard_map(
        on_device, mesh=mesh, in_specs=placed, out_specs=P(("group", "seq"), None), check_vma=False
    )
```

profile of v0, /device:TPU:3, one launch (start us, length us, event | category | flops | bytes accessed | tf_op | source)
XLA Modules:
  0.0 341.9 jit_solution(6311281531585466854)
XLA Ops:
  1.0 3.7 %collective-permute-start = (f32[128,128]{1,0:T(8,128)S(1)}, f32[128,128]{1,0:T(8,128)S(1)}, u32[]{:S(2)}, u32[]{:S(2)}) collective-permute-start(f32[128,128]{1,0:T(8,128)S(1)} %get-tuple-element.25), channel_id=1, source_target_pairs={{0,1},{1,2},{2,3},{3,4},{4,5},{5,6},{6,7},{7,8},{8,9},{9,10},{10,1... | collective-permute-start | bytes 196616 | tf_op jit(solution)/shard_map/ppermute | solution.py:22
  7.6 3.7 %collective-permute-done.1 = f32[128,128]{1,0:T(8,128)S(1)} collective-permute-done((f32[128,128]{1,0:T(8,128)S(1)}, f32[128,128]{1,0:T(8,128)S(1)}, u32[]{:S(2)}, u32[]{:S(2)}) %collective-permute-start.1) | collective-permute-done | bytes 65568 | tf_op jit(solution)/shard_map/ppermute | solution.py:23
  18.0 4.5 %collective-permute-start.2 = (f32[128,128]{1,0:T(8,128)S(1)}, f32[128,128]{1,0:T(8,128)S(1)}, u32[]{:S(2)}, u32[]{:S(2)}) collective-permute-start(f32[128,128]{1,0:T(8,128)S(1)} %bitcast.167), channel_id=1, source_target_pairs={{0,1},{1,2},{2,3},{3,4},{4,5},{5,6},{6,7},{7,8},{8,9},{9,10},{10,1... | collective-permute-start | bytes 196616 | tf_op jit(solution)/shard_map/ppermute | solution.py:22
  28.8 5.2 %collective-permute-start.4 = (f32[128,128]{1,0:T(8,128)S(1)}, f32[128,128]{1,0:T(8,128)S(1)}, u32[]{:S(2)}, u32[]{:S(2)}) collective-permute-start(f32[128,128]{1,0:T(8,128)S(1)} %get-tuple-element.21), channel_id=1, source_target_pairs={{0,1},{1,2},{2,3},{3,4},{4,5},{5,6},{6,7},{7,8},{8,9},{9,10},{10,1... | collective-permute-start | bytes 196616 | tf_op jit(solution)/shard_map/ppermute | solution.py:22
  35.9 4.5 %collective-permute-done.5 = f32[128,128]{1,0:T(8,128)S(1)} collective-permute-done((f32[128,128]{1,0:T(8,128)S(1)}, f32[128,128]{1,0:T(8,128)S(1)}, u32[]{:S(2)}, u32[]{:S(2)}) %collective-permute-start.5) | collective-permute-done | bytes 65568 | tf_op jit(solution)/shard_map/ppermute | solution.py:23
  50.3 4.1 %collective-permute-done.7 = f32[128,128]{1,0:T(8,128)S(1)} collective-permute-done((f32[128,128]{1,0:T(8,128)S(1)}, f32[128,128]{1,0:T(8,128)S(1)}, u32[]{:S(2)}, u32[]{:S(2)}) %collective-permute-start.7) | collective-permute-done | bytes 65568 | tf_op jit(solution)/shard_map/ppermute | solution.py:23
  64.2 4.1 %collective-permute-done.9 = f32[128,128]{1,0:T(8,128)S(1)} collective-permute-done((f32[128,128]{1,0:T(8,128)S(1)}, f32[128,128]{1,0:T(8,128)S(1)}, u32[]{:S(2)}, u32[]{:S(2)}) %collective-permute-start.9) | collective-permute-done | bytes 65568 | tf_op jit(solution)/shard_map/ppermute | solution.py:23
  79.0 4.1 %collective-permute-done.11 = f32[128,128]{1,0:T(8,128)S(1)} collective-permute-done((f32[128,128]{1,0:T(8,128)S(1)}, f32[128,128]{1,0:T(8,128)S(1)}, u32[]{:S(2)}, u32[]{:S(2)}) %collective-permute-start.11) | collective-permute-done | bytes 65568 | tf_op jit(solution)/shard_map/ppermute | solution.py:23
  93.8 4.1 %collective-permute-done.13 = f32[128,128]{1,0:T(8,128)S(1)} collective-permute-done((f32[128,128]{1,0:T(8,128)S(1)}, f32[128,128]{1,0:T(8,128)S(1)}, u32[]{:S(2)}, u32[]{:S(2)}) %collective-permute-start.13) | collective-permute-done | bytes 65568 | tf_op jit(solution)/shard_map/ppermute | solution.py:23
  106.2 2.6 collective-permute-start.15
  109.5 3.2 collective-permute-done.15
  118.1 7.1 %fusion.24 = bf16[512,128]{1,0:T(8,128)(2,1)S(1)} fusion(f32[512,128]{1,0:T(8,128)} %copy-done.5, f32[8,128,64]{1,2,0:T(8,128)S(1)} %fusion.21, f32[512,128]{1,0:T(8,128)} %copy-done.6, f32[512,128]{1,0:T(8,128)} %copy-done.4, f32[512,128]{1,0:T(8,128)} %copy-done.3, f32[512,128]{1,0:T(8,128)} %copy-done.2, f32[512,128]{1,0:T(8,128)S(1)} %bitcast_subtract_fusion.6, ...), kind=kLoop, calls=%fused_computation.49 | loop fusion | flops 1245184 | bytes 2490404 | tf_op jit(solution)/shard_map/convert_element_type | solution.py:66
  125.1 8.5 %convolution_convert_fusion = bf16[512,3072]{1,0:T(8,128)(2,1)} fusion(bf16[1024,3072]{1,0:T(8,128)(2,1)} %param.18, bf16[512,1024]{1,0:T(8,128)(2,1)} %param.10, bf16[512,128]{1,0:T(8,128)(2,1)S(1)} %fusion.24, bf16[128,1024]{1,0:T(8,128)(2,1)} %param.17), kind=kOutput, calls=%fused_computation.16 | convolution fusion | flops 3358588928 | bytes 10878976 | tf_op jit(solution)/shard_map/dot_general | solution.py:69
  136.9 6.1 %collective-permute-done.16 = bf16[128,2048]{1,0:T(8,128)(2,1)S(1)} collective-permute-done((bf16[128,2048]{1,0:T(8,128)(2,1)S(1)}, bf16[128,2048]{1,0:T(8,128)(2,1)S(1)}, u32[]{:S(2)}, u32[]{:S(2)}) %collective-permute-start.16) | collective-permute-done | bytes 524320 | tf_op jit(solution)/shard_map/ppermute | solution.py:22
  143.8 4.1 %fusion.27 = (bf16[512,2048]{1,0:T(8,128)(2,1)}, bf16[2816,2048]{1,0:T(8,128)(2,1)}) fusion(bf16[512,3072]{1,0:T(8,128)(2,1)} %convolution_convert_fusion, bf16[2816,2048]{1,0:T(8,128)(2,1)} %constant_dynamic-update-slice_fusion.6), kind=kLoop, calls=%fused_computation.73 | loop fusion | bytes 6291456 | tf_op jit(solution)/shard_map/slice | solution.py:71
  148.3 3.4 %collective-permute-start.20 = (bf16[512,2048]{1,0:T(8,128)(2,1)}, bf16[512,2048]{1,0:T(8,128)(2,1)}, u32[]{:S(2)}, u32[]{:S(2)}) collective-permute-start(bf16[512,2048]{1,0:T(8,128)(2,1)} %get-tuple-element.7), channel_id=1, source_target_pairs={{0,4},{1,5},{2,6},{3,7},{4,0},{5,1},{6,2},{7,3},{8,12},{9,13},{10,... | collective-permute-start | bytes 6291464 | tf_op jit(solution)/shard_map/ppermute | solution.py:31
  154.0 2.8 collective-permute-start.17
  159.3 4.0 %reshape.199 = bf16[8,64,16,64]{3,2,1,0:T(8,128)(2,1)} reshape(bf16[512,1024]{1,0:T(8,128)(2,1)} %slice.172) | data formatting | bytes 2097152 | tf_op jit(solution)/shard_map/reshape | solution.py:90
  163.3 84.8 %collective-permute-done.17 = bf16[128,2048]{1,0:T(8,128)(2,1)S(1)} collective-permute-done((bf16[128,2048]{1,0:T(8,128)(2,1)S(1)}, bf16[128,2048]{1,0:T(8,128)(2,1)S(1)}, u32[]{:S(2)}, u32[]{:S(2)}) %collective-permute-start.17) | collective-permute-done | bytes 524320 | tf_op jit(solution)/shard_map/ppermute | solution.py:23
  249.0 3.2 constant_dynamic-update-slice_fusion.3
  252.1 3.1 constant_dynamic-update-slice_fusion.2
  255.3 3.2 constant_dynamic-update-slice_fusion.1
  258.5 3.1 constant_dynamic-update-slice_fusion
  261.7 11.9 %gather_fusion.8 = bf16[64,64,2048]{2,1,0:T(8,128)(2,1)} fusion(bf16[44,64,2048]{2,1,0:T(8,128)(2,1)} %bitcast.61, s32[1024]{0:T(1024)S(1)} %pad_clamp_fusion), kind=kCustom, calls=%fused_computation.8 | custom fusion | bytes 33554688 | tf_op jit(solution)/shard_map/gather | solution.py:87
  273.6 11.7 %fusion.26 = (bf16[8,512,1024]{2,1,0:T(8,128)(2,1)}, bf16[8,512,1024]{2,1,0:T(8,128)(2,1)}) fusion(bf16[8,512,2048]{2,1,0:T(8,128)(2,1)} %bitcast.146), kind=kLoop, calls=%fused_computation.72 | loop fusion | bytes 33554432 | tf_op jit(solution)/shard_map/slice | solution.py:88
  285.2 11.4 %copy.33 = bf16[8,512,1024]{1,2,0:T(8,128)(2,1)} copy(bf16[8,512,1024]{2,1,0:T(8,128)(2,1)} %get-tuple-element.5) | data formatting | bytes 16777216
  296.7 11.4 %copy.32 = bf16[8,512,1024]{1,2,0:T(8,128)(2,1)} copy(bf16[8,512,1024]{2,1,0:T(8,128)(2,1)} %get-tuple-element.6) | data formatting | bytes 16777216
  308.1 10.9 %fusion.38 = (f32[8,16,64]{2,1,0:T(8,128)S(1)}, f32[8,16,64,512]{3,2,1,0:T(8,128)}) fusion(bf16[8,512,16,64]{1,3,2,0:T(8,128)(2,1)} %bitcast.147, bf16[8,64,16,64]{3,2,1,0:T(8,128)(2,1)} %reshape.199), kind=kOutput, calls=%fused_computation.84 | convolution fusion | flops 549454336 | bytes 26247168 | tf_op jit(solution)/shard_map/sub | solution.py:93
  319.0 11.0 %convert_bitcast_fusion = bf16[8,64,16,64]{1,3,2,0:T(8,128)(2,1)} fusion(bf16[8,512,16,64]{1,3,2,0:T(8,128)(2,1)} %bitcast.148, f32[8,16,64,512]{3,2,1,0:T(8,128)} %get-tuple-element.37, f32[8,16,64]{2,1,0:T(8,128)S(1)} %get-tuple-element.36), kind=kOutput, calls=%fused_computation.18 | convolution fusion | flops 545783808 | bytes 26247168 | tf_op jit(solution)/shard_map/bhqk,bkhd->bqhd/dot_general | solution.py:94
  329.9 4.4 %copy.23 = bf16[8,64,16,64]{3,2,1,0:T(8,128)(2,1)} copy(bf16[8,64,16,64]{1,3,2,0:T(8,128)(2,1)} %convert_bitcast_fusion) | data formatting | bytes 2097152 | tf_op jit(solution)/shard_map/convert_element_type | solution.py:95
  334.3 4.1 %convert_element_type.32 = bf16[512,1024]{1,0:T(8,128)(2,1)} reshape(bf16[8,64,16,64]{3,2,1,0:T(8,128)(2,1)} %copy.23) | data formatting | bytes 2097152 | tf_op jit(solution)/shard_map/convert_element_type | solution.py:95
  338.4 3.4 %convolution_convert_fusion.1 = bf16[512,1024]{1,0:T(8,128)(2,1)} fusion(bf16[512,1024]{1,0:T(8,128)(2,1)} %convert_element_type.32, bf16[1024,1024]{1,0:T(8,128)(2,1)S(1)} %copy-done), kind=kOutput, calls=%fused_computation.23 | convolution fusion | flops 1074266112 | bytes 4194304 | tf_op jit(solution)/shard_map/dot_general | solution.py:96
  (104 shorter events, 84.1 us)
Async XLA Ops:
  0.0 338.4 %copy-start = (bf16[1024,1024]{1,0:T(8,128)(2,1)S(1)}, bf16[1024,1024]{1,0:T(8,128)(2,1)}, u32[]{:S(2)}) copy-start(bf16[1024,1024]{1,0:T(8,128)(2,1)} %param.19) | copy-start | bytes 6291460
  0.0 43.7 %copy-start.1 = (f32[8,3,64,64]{3,2,1,0:T(8,128)S(1)}, f32[8,3,64,64]{3,2,1,0:T(8,128)}, u32[]{:S(2)}) copy-start(f32[8,3,64,64]{3,2,1,0:T(8,128)} %param.12) | copy-start | bytes 1179652
  1.0 6.5 %collective-permute-start = (f32[128,128]{1,0:T(8,128)S(1)}, f32[128,128]{1,0:T(8,128)S(1)}, u32[]{:S(2)}, u32[]{:S(2)}) collective-permute-start(f32[128,128]{1,0:T(8,128)S(1)} %get-tuple-element.25), channel_id=1, source_target_pairs={{0,1},{1,2},{2,3},{3,4},{4,5},{5,6},{6,7},{7,8},{8,9},{9,10},{10,1... | collective-permute-start | bytes 196616 | tf_op jit(solution)/shard_map/ppermute | solution.py:22
  4.8 6.5 %collective-permute-start.1 = (f32[128,128]{1,0:T(8,128)S(1)}, f32[128,128]{1,0:T(8,128)S(1)}, u32[]{:S(2)}, u32[]{:S(2)}) collective-permute-start(f32[128,128]{1,0:T(8,128)S(1)} %get-tuple-element.26), channel_id=1, source_target_pairs={{1,0},{2,1},{3,2},{4,3},{5,4},{6,5},{7,6},{8,7},{9,8},{10,9},{11,1... | collective-permute-start | bytes 196616 | tf_op jit(solution)/shard_map/ppermute | solution.py:23
  16.1 6.6 %collective-permute-start.3 = (f32[128,128]{1,0:T(8,128)S(1)}, f32[128,128]{1,0:T(8,128)S(1)}, u32[]{:S(2)}, u32[]{:S(2)}) collective-permute-start(f32[128,128]{1,0:T(8,128)S(1)} %bitcast.168), channel_id=1, source_target_pairs={{1,0},{2,1},{3,2},{4,3},{5,4},{6,5},{7,6},{8,7},{9,8},{10,9},{11,1... | collective-permute-start | bytes 196616 | tf_op jit(solution)/shard_map/ppermute | solution.py:23
  18.0 5.9 %collective-permute-start.2 = (f32[128,128]{1,0:T(8,128)S(1)}, f32[128,128]{1,0:T(8,128)S(1)}, u32[]{:S(2)}, u32[]{:S(2)}) collective-permute-start(f32[128,128]{1,0:T(8,128)S(1)} %bitcast.167), channel_id=1, source_target_pairs={{0,1},{1,2},{2,3},{3,4},{4,5},{5,6},{6,7},{7,8},{8,9},{9,10},{10,1... | collective-permute-start | bytes 196616 | tf_op jit(solution)/shard_map/ppermute | solution.py:22
  28.8 7.1 %collective-permute-start.4 = (f32[128,128]{1,0:T(8,128)S(1)}, f32[128,128]{1,0:T(8,128)S(1)}, u32[]{:S(2)}, u32[]{:S(2)}) collective-permute-start(f32[128,128]{1,0:T(8,128)S(1)} %get-tuple-element.21), channel_id=1, source_target_pairs={{0,1},{1,2},{2,3},{3,4},{4,5},{5,6},{6,7},{7,8},{8,9},{9,10},{10,1... | collective-permute-start | bytes 196616 | tf_op jit(solution)/shard_map/ppermute | solution.py:22
  34.0 6.5 %collective-permute-start.5 = (f32[128,128]{1,0:T(8,128)S(1)}, f32[128,128]{1,0:T(8,128)S(1)}, u32[]{:S(2)}, u32[]{:S(2)}) collective-permute-start(f32[128,128]{1,0:T(8,128)S(1)} %get-tuple-element.22), channel_id=1, source_target_pairs={{1,0},{2,1},{3,2},{4,3},{5,4},{6,5},{7,6},{8,7},{9,8},{10,9},{11,1... | collective-permute-start | bytes 196616 | tf_op jit(solution)/shard_map/ppermute | solution.py:23
  45.9 8.4 %copy-start.2 = (f32[512,128]{1,0:T(8,128)}, f32[512,128]{1,0:T(8,128)S(1)}, u32[]{:S(2)}) copy-start(f32[512,128]{1,0:T(8,128)S(1)} %bitcast_subtract_fusion.5) | copy-start | bytes 786436
  45.9 4.3 %collective-permute-start.6 = (f32[128,128]{1,0:T(8,128)S(1)}, f32[128,128]{1,0:T(8,128)S(1)}, u32[]{:S(2)}, u32[]{:S(2)}) collective-permute-start(f32[128,128]{1,0:T(8,128)S(1)} %get-tuple-element.19), channel_id=1, source_target_pairs={{0,1},{1,2},{2,3},{3,4},{4,5},{5,6},{6,7},{7,8},{8,9},{9,10},{10,1... | collective-permute-start | bytes 196616 | tf_op jit(solution)/shard_map/ppermute | solution.py:22
  47.8 6.5 %collective-permute-start.7 = (f32[128,128]{1,0:T(8,128)S(1)}, f32[128,128]{1,0:T(8,128)S(1)}, u32[]{:S(2)}, u32[]{:S(2)}) collective-permute-start(f32[128,128]{1,0:T(8,128)S(1)} %get-tuple-element.20), channel_id=1, source_target_pairs={{1,0},{2,1},{3,2},{4,3},{5,4},{6,5},{7,6},{8,7},{9,8},{10,9},{11,1... | collective-permute-start | bytes 196616 | tf_op jit(solution)/shard_map/ppermute | solution.py:23
  59.7 49.1 %copy-start.7 = (f32[9]{0:T(128)S(1)}, f32[9]{0:T(128)}, u32[]{:S(2)}) copy-start(f32[9]{0:T(128)} %param.16) | copy-start | bytes 112
  59.8 8.4 %copy-start.3 = (f32[512,128]{1,0:T(8,128)}, f32[512,128]{1,0:T(8,128)S(1)}, u32[]{:S(2)}) copy-start(f32[512,128]{1,0:T(8,128)S(1)} %bitcast_subtract_fusion.4) | copy-start | bytes 786436
  59.8 4.3 %collective-permute-start.8 = (f32[128,128]{1,0:T(8,128)S(1)}, f32[128,128]{1,0:T(8,128)S(1)}, u32[]{:S(2)}, u32[]{:S(2)}) collective-permute-start(f32[128,128]{1,0:T(8,128)S(1)} %get-tuple-element.17), channel_id=1, source_target_pairs={{0,1},{1,2},{2,3},{3,4},{4,5},{5,6},{6,7},{7,8},{8,9},{9,10},{10,1... | collective-permute-start | bytes 196616 | tf_op jit(solution)/shard_map/ppermute | solution.py:22
  61.7 6.5 %collective-permute-start.9 = (f32[128,128]{1,0:T(8,128)S(1)}, f32[128,128]{1,0:T(8,128)S(1)}, u32[]{:S(2)}, u32[]{:S(2)}) collective-permute-start(f32[128,128]{1,0:T(8,128)S(1)} %get-tuple-element.18), channel_id=1, source_target_pairs={{1,0},{2,1},{3,2},{4,3},{5,4},{6,5},{7,6},{8,7},{9,8},{10,9},{11,1... | collective-permute-start | bytes 196616 | tf_op jit(solution)/shard_map/ppermute | solution.py:23
  74.6 8.4 %copy-start.4 = (f32[512,128]{1,0:T(8,128)}, f32[512,128]{1,0:T(8,128)S(1)}, u32[]{:S(2)}) copy-start(f32[512,128]{1,0:T(8,128)S(1)} %bitcast_subtract_fusion.3) | copy-start | bytes 786436
  74.6 4.3 %collective-permute-start.10 = (f32[128,128]{1,0:T(8,128)S(1)}, f32[128,128]{1,0:T(8,128)S(1)}, u32[]{:S(2)}, u32[]{:S(2)}) collective-permute-start(f32[128,128]{1,0:T(8,128)S(1)} %get-tuple-element.15), channel_id=1, source_target_pairs={{0,1},{1,2},{2,3},{3,4},{4,5},{5,6},{6,7},{7,8},{8,9},{9,10},{10,1... | collective-permute-start | bytes 196616 | tf_op jit(solution)/shard_map/ppermute | solution.py:22
  76.6 6.5 %collective-permute-start.11 = (f32[128,128]{1,0:T(8,128)S(1)}, f32[128,128]{1,0:T(8,128)S(1)}, u32[]{:S(2)}, u32[]{:S(2)}) collective-permute-start(f32[128,128]{1,0:T(8,128)S(1)} %get-tuple-element.16), channel_id=1, source_target_pairs={{1,0},{2,1},{3,2},{4,3},{5,4},{6,5},{7,6},{8,7},{9,8},{10,9},{11,1... | collective-permute-start | bytes 196616 | tf_op jit(solution)/shard_map/ppermute | solution.py:23
  89.4 8.4 %copy-start.5 = (f32[512,128]{1,0:T(8,128)}, f32[512,128]{1,0:T(8,128)S(1)}, u32[]{:S(2)}) copy-start(f32[512,128]{1,0:T(8,128)S(1)} %bitcast_subtract_fusion.2) | copy-start | bytes 786436
  89.5 4.3 %collective-permute-start.12 = (f32[128,128]{1,0:T(8,128)S(1)}, f32[128,128]{1,0:T(8,128)S(1)}, u32[]{:S(2)}, u32[]{:S(2)}) collective-permute-start(f32[128,128]{1,0:T(8,128)S(1)} %get-tuple-element.13), channel_id=1, source_target_pairs={{0,1},{1,2},{2,3},{3,4},{4,5},{5,6},{6,7},{7,8},{8,9},{9,10},{10,1... | collective-permute-start | bytes 196616 | tf_op jit(solution)/shard_map/ppermute | solution.py:22
  91.4 6.5 %collective-permute-start.13 = (f32[128,128]{1,0:T(8,128)S(1)}, f32[128,128]{1,0:T(8,128)S(1)}, u32[]{:S(2)}, u32[]{:S(2)}) collective-permute-start(f32[128,128]{1,0:T(8,128)S(1)} %get-tuple-element.14), channel_id=1, source_target_pairs={{1,0},{2,1},{3,2},{4,3},{5,4},{6,5},{7,6},{8,7},{9,8},{10,9},{11,1... | collective-permute-start | bytes 196616 | tf_op jit(solution)/shard_map/ppermute | solution.py:23
  104.2 8.4 %copy-start.6 = (f32[512,128]{1,0:T(8,128)}, f32[512,128]{1,0:T(8,128)S(1)}, u32[]{:S(2)}) copy-start(f32[512,128]{1,0:T(8,128)S(1)} %bitcast_subtract_fusion.1) | copy-start | bytes 786436
  104.3 5.2 %collective-permute-start.14 = (f32[128,128]{1,0:T(8,128)S(1)}, f32[128,128]{1,0:T(8,128)S(1)}, u32[]{:S(2)}, u32[]{:S(2)}) collective-permute-start(f32[128,128]{1,0:T(8,128)S(1)} %get-tuple-element.11), channel_id=1, source_target_pairs={{0,1},{1,2},{2,3},{3,4},{4,5},{5,6},{6,7},{7,8},{8,9},{9,10},{10,1... | collective-permute-start | bytes 196616 | tf_op jit(solution)/shard_map/ppermute | solution.py:22
  106.2 6.5 %collective-permute-start.15 = (f32[128,128]{1,0:T(8,128)S(1)}, f32[128,128]{1,0:T(8,128)S(1)}, u32[]{:S(2)}, u32[]{:S(2)}) collective-permute-start(f32[128,128]{1,0:T(8,128)S(1)} %get-tuple-element.12), channel_id=1, source_target_pairs={{1,0},{2,1},{3,2},{4,3},{5,4},{6,5},{7,6},{8,7},{9,8},{10,9},{11,1... | collective-permute-start | bytes 196616 | tf_op jit(solution)/shard_map/ppermute | solution.py:23
  133.7 20.4 %copy-start.8 = (s32[8,3]{0,1:T(4,128)S(1)}, s32[8,3]{0,1:T(4,128)}, u32[]{:S(2)}) copy-start(s32[8,3]{0,1:T(4,128)} %param.14) | copy-start | bytes 292
  133.7 23.1 %copy-start.9 = (s32[8,4]{0,1:T(4,128)S(1)}, s32[8,4]{0,1:T(4,128)}, u32[]{:S(2)}) copy-start(s32[8,4]{0,1:T(4,128)} %param.15) | copy-start | bytes 388
  135.0 8.0 %collective-permute-start.16 = (bf16[128,2048]{1,0:T(8,128)(2,1)S(1)}, bf16[128,2048]{1,0:T(8,128)(2,1)S(1)}, u32[]{:S(2)}, u32[]{:S(2)}) collective-permute-start(bf16[128,2048]{1,0:T(8,128)(2,1)S(1)} %get-tuple-element.10), channel_id=1, source_target_pairs={{0,1},{1,2},{2,3},{3,4},{4,5},{5,6},{6,7},{7,8},{8,9},{9,10},{10,1... | collective-permute-start | bytes 1572872 | tf_op jit(solution)/shard_map/ppermute | solution.py:22
  147.9 101.0 %collective-permute-start.18 = (bf16[512,2048]{1,0:T(8,128)(2,1)}, bf16[512,2048]{1,0:T(8,128)(2,1)}, u32[]{:S(2)}, u32[]{:S(2)}) collective-permute-start(bf16[512,2048]{1,0:T(8,128)(2,1)} %get-tuple-element.7), channel_id=1, source_target_pairs={{0,1},{1,0},{2,3},{3,2},{4,5},{5,4},{6,7},{7,6},{8,9},{9,8},{10,11... | collective-permute-start | bytes 6291464 | tf_op jit(solution)/shard_map/ppermute | solution.py:31
  148.3 103.9 %collective-permute-start.19 = (bf16[512,2048]{1,0:T(8,128)(2,1)}, bf16[512,2048]{1,0:T(8,128)(2,1)}, u32[]{:S(2)}, u32[]{:S(2)}) collective-permute-start(bf16[512,2048]{1,0:T(8,128)(2,1)} %get-tuple-element.7), channel_id=1, source_target_pairs={{0,2},{1,3},{2,0},{3,1},{4,6},{5,7},{6,4},{7,5},{8,10},{9,11},{10,... | collective-permute-start | bytes 6291464 | tf_op jit(solution)/shard_map/ppermute | solution.py:31
  148.3 107.0 %collective-permute-start.20 = (bf16[512,2048]{1,0:T(8,128)(2,1)}, bf16[512,2048]{1,0:T(8,128)(2,1)}, u32[]{:S(2)}, u32[]{:S(2)}) collective-permute-start(bf16[512,2048]{1,0:T(8,128)(2,1)} %get-tuple-element.7), channel_id=1, source_target_pairs={{0,4},{1,5},{2,6},{3,7},{4,0},{5,1},{6,2},{7,3},{8,12},{9,13},{10,... | collective-permute-start | bytes 6291464 | tf_op jit(solution)/shard_map/ppermute | solution.py:31
  151.7 106.8 %collective-permute-start.21 = (bf16[512,2048]{1,0:T(8,128)(2,1)}, bf16[512,2048]{1,0:T(8,128)(2,1)}, u32[]{:S(2)}, u32[]{:S(2)}) collective-permute-start(bf16[512,2048]{1,0:T(8,128)(2,1)} %get-tuple-element.7), channel_id=1, source_target_pairs={{0,8},{1,9},{2,10},{3,11},{4,12},{5,13},{6,14},{7,15},{8,0},{9,1},... | collective-permute-start | bytes 6291464 | tf_op jit(solution)/shard_map/ppermute | solution.py:31
  154.0 94.1 %collective-permute-start.17 = (bf16[128,2048]{1,0:T(8,128)(2,1)S(1)}, bf16[128,2048]{1,0:T(8,128)(2,1)S(1)}, u32[]{:S(2)}, u32[]{:S(2)}) collective-permute-start(bf16[128,2048]{1,0:T(8,128)(2,1)S(1)} %get-tuple-element.9), channel_id=1, source_target_pairs={{1,0},{2,1},{3,2},{4,3},{5,4},{6,5},{7,6},{8,7},{9,8},{10,9},{11,1... | collective-permute-start | bytes 1572872 | tf_op jit(solution)/shard_map/ppermute | solution.py:23
where the time goes:
time: 346 us; the launch traced here: 342 us
  waiting for transfers between devices  120 us (35%)
  local copies, waits for them, and re-layouts  101 us (29%)
  starting transfers between devices  51.8 us (15%)
  matrix products  51.4 us (15%)
  other arithmetic  17.5 us (5%)
    ppermute x9, waiting for transfers between devices, extended(): after = lax.ppermute(first, axis, down)  113 us
    unnamed x27, local copies, waits for them, and re-layouts  34.1 us
    ppermute x9, starting transfers between devices, extended(): before = lax.ppermute(last, axis, up)  25 us
    ppermute x9, starting transfers between devices, extended(): after = lax.ppermute(first, axis, down)  20.7 us
    gather x8, local copies, waits for them, and re-layouts, apply_operator(): picked = pooled[position]  17.8 us
    dot_general x8, matrix products, apply_operator(): jnp.einsum('bjst,bjtc->bsc', op_blocks, picked, precision=lax.Precision.H...  17.6 us
    gather x1, local copies, waits for them, and re-layouts, on_device(): picked = pool_blocks[key_slots].reshape(count, -1, 2 * D)  11.9 us
    slice x1, local copies, waits for them, and re-layouts, on_device(): keys = picked[:, :, :D].reshape(count, -1, HEADS, HD)  11.7 us
  transfers between devices with their start and end apart: 22, of which 11 were waited for; matrix products, arithmetic and copies ran while one was open for 5% of the time, Pallas kernels for 0%

commit v1 on v0

v1 whole, which is shorter than its diff:
```python
import functools

import jax
import jax.numpy as jnp
from jax import lax
from jax.experimental import pallas as pl
from jax.experimental.pallas import tpu as pltpu
from jax.sharding import PartitionSpec as P

D = 1024
HEADS = 16
HD = 64
BS = 64
DEG = 8
NEXP = 4
REACH = 2
NL = 3
MESH = pl.DeviceIdType.MESH
F32, BF16 = jnp.float32, jnp.bfloat16
VMEM_LIMIT = 56 * 1024 * 1024


def split(x):
    hi = x.astype(BF16)
    lo = (x - hi.astype(F32)).astype(BF16)
    return jnp.concatenate([hi, lo], axis=-1)


def diffuse_kernel(
    n,
    node_ref,
    struct_ref,
    ops_ref,
    lap_ref,
    coef_ref,
    npool_ref,
    epool_ref,
    pool,
    halo,
    terms,
    enc,
    opcat,
    hsend,
    hrecv,
    nsend,
    nrecv,
    esend,
    erecv,
    own_sem,
):
    count = ops_ref.shape[0]
    rows = count * BS
    rim = REACH * BS
    me = lax.axis_index("seq")
    has_left, has_right = me > 0, me < n - 1
    levels = n.bit_length() - 1
    partners = []
    for link in range(NEXP):
        mask = 2 ** (link * (levels - 1) // (NEXP - 1))
        bit = lax.rem(me // mask, 2)
        partners.append(me + mask * (1 - 2 * bit))

    barrier = pltpu.get_barrier_semaphore()
    for peer in partners:
        pl.semaphore_signal(barrier, inc=1, device_id={"seq": peer}, device_id_type=MESH)

    @pl.when(has_left)
    def _():
        pl.semaphore_signal(barrier, inc=1, device_id={"seq": me - 1}, device_id_type=MESH)

    @pl.when(has_right)
    def _():
        pl.semaphore_signal(barrier, inc=1, device_id={"seq": me + 1}, device_id_type=MESH)

    t0 = struct_ref[...]
    terms[0] = t0.reshape(count, BS, -1)
    terms[1] = jnp.zeros_like(terms[1])
    enc[...] = coef_ref[0] * t0.reshape(count, BS, -1)
    pool[0, REACH : REACH + count] = split(t0).reshape(count, BS, -1)
    peers = NEXP + has_left.astype(jnp.int32) + has_right.astype(jnp.int32)
    pl.semaphore_wait(barrier, peers)

    def to_left(src, dst, send, recv):
        return pltpu.make_async_remote_copy(
            src, dst, send, recv, device_id={"seq": me - 1}, device_id_type=MESH
        )

    def to_right(src, dst, send, recv):
        return pltpu.make_async_remote_copy(
            src, dst, send, recv, device_id={"seq": me + 1}, device_id_type=MESH
        )

    def halo_left(k):
        return to_left(
            pool.at[lax.rem(k, 2), pl.ds(REACH, REACH)], halo.at[k, 1], hsend.at[k, 0], hrecv.at[k, 1]
        )

    def halo_right(k):
        return to_right(
            pool.at[lax.rem(k, 2), pl.ds(count, REACH)], halo.at[k, 0], hsend.at[k, 1], hrecv.at[k, 0]
        )

    def start_halo(k):
        @pl.when(has_left)
        def _():
            halo_left(k).start()

        @pl.when(has_right)
        def _():
            halo_right(k).start()

    def wait_halo(k):
        @pl.when(has_left)
        def _():
            halo_right(k).wait_recv()
            pool[lax.rem(k, 2), 0:REACH] = halo[k, 0]

        @pl.when(has_right)
        def _():
            halo_left(k).wait_recv()
            pool[lax.rem(k, 2), count + REACH :] = halo[k, 1]

    def wait_halo_sent(k):
        @pl.when(has_left)
        def _():
            halo_left(k).wait_send()

        @pl.when(has_right)
        def _():
            halo_right(k).wait_send()

    start_halo(0)

    def near_left(src, dst, width_rows, send, recv):
        return to_left(src.at[pl.ds(0, rim)], dst.at[pl.ds(rim + width_rows, rim)], send.at[NEXP], recv.at[NEXP])

    def near_right(src, dst, width_rows, send, recv):
        return to_right(
            src.at[pl.ds(width_rows - rim, rim)], dst.at[pl.ds(0, rim)], send.at[NEXP + 1], recv.at[NEXP + 1]
        )

    def far(src, dst, link, send, recv):
        return pltpu.make_async_remote_copy(
            src,
            dst.at[pl.ds(2 * rim + rows + link * rows, rows)],
            send.at[link],
            recv.at[link],
            device_id={"seq": partners[link]},
            device_id_type=MESH,
        )

    def start_pool(src, dst, send, recv):
        for link in reversed(range(NEXP)):
            far(src, dst, link, send, recv).start()

        @pl.when(has_left)
        def _():
            near_left(src, dst, rows, send, recv).start()

        @pl.when(has_right)
        def _():
            near_right(src, dst, rows, send, recv).start()

    def wait_pool(src, dst, send, recv):
        for link in range(NEXP):
            copy = far(src, dst, link, send, recv)
            copy.wait_send()
            copy.wait_recv()

        @pl.when(has_left)
        def _():
            near_left(src, dst, rows, send, recv).wait_send()
            near_right(src, dst, rows, send, recv).wait_recv()

        @pl.when(has_right)
        def _():
            near_right(src, dst, rows, send, recv).wait_send()
            near_left(src, dst, rows, send, recv).wait_recv()

    start_pool(node_ref, npool_ref, nsend, nrecv)
    own_copy = pltpu.make_async_copy(node_ref, npool_ref.at[pl.ds(rim, rows)], own_sem)
    own_copy.start()

    for b in range(count):
        wide = jnp.concatenate([ops_ref[b, j] for j in range(NL)], axis=1)
        hi = wide.astype(BF16)
        opcat[b, 0:BS] = hi
        opcat[b, BS : 2 * BS] = (wide - hi.astype(F32)).astype(BF16)

    first = me * count - REACH

    def step(k, carry):
        now, before = lax.rem(k, 2), lax.rem(k + 1, 2)
        factor = jnp.where(k == 1, 1.0, 2.0).astype(F32)

        def block(b):
            picked = jnp.concatenate(
                [pool[before, jnp.clip(lap_ref[b, j] - first, 0, count + 2 * REACH - 1)] for j in range(NL)],
                axis=0,
            )
            r = jnp.dot(opcat[b], picked, preferred_element_type=F32)
            r = r[:BS] + r[BS:]
            r = r[:, : r.shape[1] // 2] + r[:, r.shape[1] // 2 :]
            new = factor * r - terms[now, b]
            terms[now, b] = new
            enc[b] = enc[b] + coef_ref[k] * new
            pool[now, REACH + b] = split(new)

        wait_halo(k - 1)

        @pl.when(k >= 2)
        def _():
            wait_halo_sent(k - 2)

        for b in [*range(REACH), *range(count - REACH, count)]:
            block(b)

        @pl.when(k < DEG)
        def _():
            start_halo(k)

        for b in range(REACH, count - REACH):
            block(b)
        return carry

    lax.fori_loop(1, DEG + 1, step, 0)
    wait_halo_sent(DEG - 1)

    epool_ref[pl.ds(rim, rows)] = enc[...].reshape(rows, -1).astype(BF16)
    own_enc = epool_ref.at[pl.ds(rim, rows)]
    start_pool(own_enc, epool_ref, esend, erecv)
    wait_pool(own_enc, epool_ref, esend, erecv)
    wait_pool(node_ref, npool_ref, nsend, nrecv)
    own_copy.wait()


def attend_kernel(count, slots_ref, npool_ref, epool_ref, we_ref, wqkv_ref, wo_ref, out_ref, blended, kv, qs, att):
    rim = REACH * BS
    chunk = 256
    total = npool_ref.shape[0] // chunk

    def project(c, carry):
        at = pl.ds(pl.multiple_of(c * chunk, chunk), chunk)
        x = jnp.dot(epool_ref[at], we_ref[...], preferred_element_type=F32)
        x = (npool_ref[at].astype(F32) + x).astype(BF16)
        blended[at] = x
        for t in range(4):
            cols = pl.ds(D + t * 512, 512)
            y = jnp.dot(x, wqkv_ref[:, cols], preferred_element_type=F32).astype(BF16)
            kv[pl.ds(c * (chunk // BS), chunk // BS), :, t * 512 : (t + 1) * 512] = y.reshape(chunk // BS, BS, 512)
        return carry

    lax.fori_loop(0, total, project, 0)

    def queries(c, carry):
        at = pl.ds(pl.multiple_of(c * chunk, chunk), chunk)
        x = blended[pl.ds(pl.multiple_of(rim + c * chunk, 128), chunk)]
        for t in range(2):
            cols = pl.ds(t * 512, 512)
            y = jnp.dot(x, wqkv_ref[:, cols], preferred_element_type=F32).astype(BF16)
            qs[at, t * 512 : (t + 1) * 512] = y * jnp.array(1.0 / HD**0.5, BF16)
        return carry

    lax.fori_loop(0, count * BS // chunk, queries, 0)

    pack = 4
    width = pack * HD
    head = lax.broadcasted_iota(jnp.int32, (BS, width), 1) // HD
    keep = [head == h for h in range(pack)]

    def attend(b, carry):
        at = pl.ds(pl.multiple_of(b * BS, BS), BS)
        where = [slots_ref[b, j] for j in range(1 + NL + NEXP)]
        for g in range(HEADS // pack):
            cols = slice(g * width, (g + 1) * width)
            vcols = slice(D + g * width, D + (g + 1) * width)
            q = qs[at, cols]
            q = jnp.concatenate([jnp.where(m, q, jnp.zeros_like(q)) for m in keep], axis=0)
            k = jnp.concatenate([kv[w, :, cols] for w in where], axis=0)
            v = jnp.concatenate([kv[w, :, vcols] for w in where], axis=0)
            s = lax.dot_general(q, k, (((1,), (1,)), ((), ())), preferred_element_type=F32)
            p = jnp.exp(s - jnp.max(s, axis=1, keepdims=True))
            p = (p * (1.0 / jnp.sum(p, axis=1, keepdims=True))).astype(BF16)
            o = jnp.dot(p, v, preferred_element_type=F32)
            mine = o[0:BS]
            for h in range(1, pack):
                mine = jnp.where(keep[h], o[h * BS : (h + 1) * BS], mine)
            att[at, cols] = mine.astype(BF16)
        return carry

    lax.fori_loop(0, count, attend, 0)

    def output(c, carry):
        at = pl.ds(pl.multiple_of(c * chunk, chunk), chunk)
        x = att[at]
        for t in range(2):
            cols = slice(t * 512, (t + 1) * 512)
            out_ref[at, cols] = jnp.dot(x, wo_ref[:, cols], preferred_element_type=F32).astype(BF16)
        return carry

    lax.fori_loop(0, count * BS // chunk, output, 0)


def on_device(
    n,
    node_feats,
    struct_feats,
    op_blocks,
    laplace_index,
    graph_links,
    expander_slot,
    series_coef,
    encode_weight,
    qkv_weight,
    out_weight,
):
    count = op_blocks.shape[0]
    rows, rim, pch = count * BS, REACH * BS, struct_feats.shape[1]
    pool_rows = rows * (1 + NEXP) + 2 * rim
    vmem = pl.BlockSpec(memory_space=pltpu.VMEM)
    smem = pl.BlockSpec(memory_space=pltpu.SMEM)
    hbm = pl.BlockSpec(memory_space=pl.ANY)
    dma = pltpu.SemaphoreType.DMA
    npool, epool = pl.pallas_call(
        functools.partial(diffuse_kernel, n),
        out_shape=(
            jax.ShapeDtypeStruct((pool_rows, D), BF16),
            jax.ShapeDtypeStruct((pool_rows, pch), BF16),
        ),
        in_specs=[hbm, vmem, vmem, smem, smem],
        out_specs=(hbm, vmem),
        scratch_shapes=[
            pltpu.VMEM((2, count + 2 * REACH, BS, 2 * pch), BF16),
            pltpu.VMEM((DEG, 2, REACH, BS, 2 * pch), BF16),
            pltpu.VMEM((2, count, BS, pch), F32),
            pltpu.VMEM((count, BS, pch), F32),
            pltpu.VMEM((count, 2 * BS, NL * BS), BF16),
            dma((DEG, 2)),
            dma((DEG, 2)),
            dma((NEXP + 2,)),
            dma((NEXP + 2,)),
            dma((NEXP + 2,)),
            dma((NEXP + 2,)),
            dma,
        ],
        compiler_params=pltpu.CompilerParams(
            collective_id=0, has_side_effects=True, vmem_limit_bytes=VMEM_LIMIT
        ),
    )(node_feats, struct_feats, op_blocks, laplace_index, series_coef)

    first_block = lax.axis_index("seq") * count
    own_slot = jnp.arange(count, dtype=jnp.int32)[:, None] + REACH
    graph_slot = graph_links - first_block + REACH
    far_base = count + 2 * REACH + jnp.arange(NEXP, dtype=jnp.int32) * count
    slots = jnp.concatenate([own_slot, graph_slot, far_base[None, :] + expander_slot], axis=1)
    return pl.pallas_call(
        functools.partial(attend_kernel, count),
        out_shape=jax.ShapeDtypeStruct((rows, D), BF16),
        in_specs=[smem, vmem, vmem, vmem, vmem, vmem],
        out_specs=vmem,
        scratch_shapes=[
            pltpu.VMEM((pool_rows, D), BF16),
            pltpu.VMEM((pool_rows // BS, BS, 2 * D), BF16),
            pltpu.VMEM((rows, D), BF16),
            pltpu.VMEM((rows, D), BF16),
        ],
        compiler_params=pltpu.CompilerParams(vmem_limit_bytes=VMEM_LIMIT),
    )(slots, npool, epool, encode_weight, qkv_weight, out_weight)


def solution(mesh):
    placed = (
        P(("group", "seq"), None),
        P(("group", "seq"), None),
        P(("group", "seq"), None, None, None),
        P(("group", "seq"), None),
        P(("group", "seq"), None),
        P(("group", "seq"), None),
        P(),
        P(),
        P(),
        P(),
    )
    return jax.shard_map(
        functools.partial(on_device, mesh.shape["seq"]),
        mesh=mesh,
        in_specs=placed,
        out_specs=P(("group", "seq"), None),
        check_vma=False,
    )
```

time: 346 us -> 129 us (0.37)
  Pallas kernels: 0 us -> 124 us
  waiting for transfers between devices: 120 us -> 0 us
  local copies, waits for them, and re-layouts: 101 us -> 2.86 us
  starting transfers between devices: 51.8 us -> 0 us
  matrix products: 51.4 us -> 0 us
  other arithmetic: 17.5 us -> 0.69 us
    pallas_call x0 -> x2, Pallas kernels: none -> 124 us  [the longest x1 88.4 us: on_device(): pl.pallas_call(functools.partial(diffuse_kernel, n), out_shape=(jax.Shape...]
    ppermute x22 -> x0, waiting for transfers between devices: 120 us -> none  [the longest x9 113 us: extended(): after = lax.ppermute(first, axis, down)]
    ppermute x22 -> x0, starting transfers between devices: 51.8 us -> none  [the longest x9 25 us: extended(): before = lax.ppermute(last, axis, up)]
    dot_general x11 -> x0, matrix products: 40.5 us -> none  [the longest x8 17.6 us: apply_operator(): jnp.einsum('bjst,bjtc->bsc', op_blocks, picked, precision=lax.Precision.H...]
    unnamed x27 -> x3, local copies, waits for them, and re-layouts: 34.1 us -> 2.86 us
    gather x9 -> x0, local copies, waits for them, and re-layouts: 29.7 us -> none  [the longest x8 17.8 us: apply_operator(): picked = pooled[position]]
    slice x13 -> x0, local copies, waits for them, and re-layouts: 21.1 us -> none  [the longest x1 11.7 us: on_device(): keys = picked[:, :, :D].reshape(count, -1, HEADS, HD)]
    sub x1 -> x0, matrix products: 10.9 us -> none  [on_device(): weights = jax.nn.softmax(scores, axis=-1).astype(jnp.bfloat16)]
  transfers between devices with their start and end apart: 22 -> 0, of which waited for: 11 -> 0; matrix products, arithmetic and copies ran while one was open for 5% -> 0% of each run, Pallas kernels for 0% -> 0%
where the time goes in v1:
time: 129 us; the launch traced here: 127 us
  Pallas kernels  124 us (96%)
  local copies, waits for them, and re-layouts  2.86 us (2%)
    pallas_call x1, Pallas kernels, on_device(): pl.pallas_call(functools.partial(diffuse_kernel, n), out_shape=(jax.Shape...  88.4 us
    pallas_call x1, Pallas kernels, on_device(): pl.pallas_call(functools.partial(attend_kernel, count), out_shape=jax.Sha...  35.2 us
    unnamed x3, local copies, waits for them, and re-layouts  2.86 us

profile of v1, /device:TPU:3, one launch (start us, length us, event | category | flops | bytes accessed | tf_op | source)
XLA Modules:
  0.0 127.2 jit_solution(2818636601664528349)
XLA Ops:
  0.0 1.3 %copy.13.lap_ref = s32[8,3]{1,0:T(8,128)} copy(s32[8,3]{0,1:T(4,128)} %param.13) | data formatting | bytes 192 | tf_op args[3]
  1.4 0.8 copy.11
  2.1 0.8 copy.12
  2.9 0.7 pad_add_fusion.slots_ref
  3.6 88.4 %shard_map.100 = (bf16[2816,1024]{1,0:T(8,128)(2,1)}, bf16[2816,128]{1,0:T(8,128)(2,1)}) custom-call(bf16[512,1024]{1,0:T(8,128)(2,1)} %node_ref.1, f32[512,128]{1,0:T(8,128)} %struct_ref.1, f32[8,3,64,64]{3,2,1,0:T(8,128)} %ops_ref.1, s32[8,3]{1,0:T(8,128)} %copy.13.lap_ref, f32[9]{0:T(128)} %coef_ref.1), custom_call_target="tpu_custom_call" | custom-call | tf_op jit(solution)/shard_map/pallas_call | solution.py:324
  92.0 35.2 %shard_map.101 = bf16[512,1024]{1,0:T(8,128)(2,1)} custom-call(s32[8,8]{1,0:T(8,128)} %pad_add_fusion.slots_ref, bf16[2816,1024]{1,0:T(8,128)(2,1)} %get-tuple-element.7.npool_ref, bf16[2816,128]{1,0:T(8,128)(2,1)} %get-tuple-element.8.epool_ref, bf16[128,1024]{1,0:T(8,128)(2,1)} %we_ref.1, bf16[1024,3072]{1,0:T(8,128)(2,1)} %wqkv_ref.1, ...), custom_call_target="tpu_custom_call" | custom-call | tf_op jit(solution)/shard_map/pallas_call | solution.py:356
  (4 shorter events, 0.0 us)

commit v2 on v1

v2 whole, which is shorter than its diff:
```python
import functools

import jax
import jax.numpy as jnp
from jax import lax
from jax.experimental import pallas as pl
from jax.experimental.pallas import tpu as pltpu
from jax.sharding import PartitionSpec as P

D = 1024
HEADS = 16
HD = 64
BS = 64
DEG = 8
NEXP = 4
REACH = 2
NL = 3
MESH = pl.DeviceIdType.MESH
F32, BF16 = jnp.float32, jnp.bfloat16
VMEM_LIMIT = 56 * 1024 * 1024


def split(x):
    hi = x.astype(BF16)
    lo = (x - hi.astype(F32)).astype(BF16)
    return jnp.concatenate([hi, lo], axis=-1)


def layer_kernel(
    n,
    node_ref,
    struct_ref,
    ops_ref,
    lap_ref,
    slots_ref,
    coef_ref,
    we_hbm,
    wqkv_hbm,
    wo_hbm,
    out_ref,
    pool0,
    pool1,
    halo,
    term0,
    term1,
    enc,
    opcat,
    npool_ref,
    epool_ref,
    we_ref,
    wqkv_ref,
    wo_ref,
    blended,
    kv,
    qs,
    att,
    hsend,
    hrecv,
    nsend,
    nrecv,
    esend,
    erecv,
    own_sem,
):
    count = ops_ref.shape[0]
    rows = count * BS
    rim = REACH * BS
    me = lax.axis_index("seq")
    has_left, has_right = me > 0, me < n - 1
    levels = n.bit_length() - 1
    partners = []
    for link in range(NEXP):
        mask = 2 ** (link * (levels - 1) // (NEXP - 1))
        bit = lax.rem(me // mask, 2)
        partners.append(me + mask * (1 - 2 * bit))

    barrier = pltpu.get_barrier_semaphore()
    for peer in partners:
        pl.semaphore_signal(barrier, inc=1, device_id={"seq": peer}, device_id_type=MESH)

    @pl.when(has_left)
    def _():
        pl.semaphore_signal(barrier, inc=1, device_id={"seq": me - 1}, device_id_type=MESH)

    @pl.when(has_right)
    def _():
        pl.semaphore_signal(barrier, inc=1, device_id={"seq": me + 1}, device_id_type=MESH)

    own_copies = [
        pltpu.make_async_copy(node_ref, npool_ref.at[pl.ds(rim, rows)], own_sem.at[0]),
        pltpu.make_async_copy(we_hbm, we_ref, own_sem.at[1]),
        pltpu.make_async_copy(wqkv_hbm, wqkv_ref, own_sem.at[2]),
        pltpu.make_async_copy(wo_hbm, wo_ref, own_sem.at[3]),
    ]
    t0 = struct_ref[...]
    term0[...] = t0.reshape(count, BS, -1)
    term1[...] = jnp.zeros_like(term1)
    enc[...] = coef_ref[0] * t0.reshape(count, BS, -1)
    pool0[REACH : REACH + count] = split(t0).reshape(count, BS, -1)
    peers = NEXP + has_left.astype(jnp.int32) + has_right.astype(jnp.int32)
    pl.semaphore_wait(barrier, peers)

    def to_left(src, dst, send, recv):
        return pltpu.make_async_remote_copy(
            src, dst, send, recv, device_id={"seq": me - 1}, device_id_type=MESH
        )

    def to_right(src, dst, send, recv):
        return pltpu.make_async_remote_copy(
            src, dst, send, recv, device_id={"seq": me + 1}, device_id_type=MESH
        )

    pools, terms = (pool0, pool1), (term0, term1)

    def halo_left(k, par):
        return to_left(pools[par].at[pl.ds(REACH, REACH)], halo.at[k, 1], hsend.at[k, 0], hrecv.at[k, 1])

    def halo_right(k, par):
        return to_right(pools[par].at[pl.ds(count, REACH)], halo.at[k, 0], hsend.at[k, 1], hrecv.at[k, 0])

    def start_halo(k, par):
        @pl.when(has_left)
        def _():
            halo_left(k, par).start()

        @pl.when(has_right)
        def _():
            halo_right(k, par).start()

    def wait_halo(k, par):
        @pl.when(has_left)
        def _():
            halo_right(k, par).wait_recv()
            pools[par][0:REACH] = halo[k, 0]

        @pl.when(has_right)
        def _():
            halo_left(k, par).wait_recv()
            pools[par][count + REACH :] = halo[k, 1]

    def wait_halo_sent(k, par):
        @pl.when(has_left)
        def _():
            halo_left(k, par).wait_send()

        @pl.when(has_right)
        def _():
            halo_right(k, par).wait_send()

    start_halo(0, 0)

    def near_left(src, dst, width_rows, send, recv):
        return to_left(src.at[pl.ds(0, rim)], dst.at[pl.ds(rim + width_rows, rim)], send.at[NEXP], recv.at[NEXP])

    def near_right(src, dst, width_rows, send, recv):
        return to_right(
            src.at[pl.ds(width_rows - rim, rim)], dst.at[pl.ds(0, rim)], send.at[NEXP + 1], recv.at[NEXP + 1]
        )

    def far(src, dst, link, send, recv, start=0, size=rows):
        return pltpu.make_async_remote_copy(
            src.at[pl.ds(start, size)],
            dst.at[pl.ds(2 * rim + rows + link * rows + start, size)],
            send.at[link],
            recv.at[link],
            device_id={"seq": partners[link]},
            device_id_type=MESH,
        )

    def start_near(src, dst, send, recv):
        @pl.when(has_left)
        def _():
            near_left(src, dst, rows, send, recv).start()

        @pl.when(has_right)
        def _():
            near_right(src, dst, rows, send, recv).start()

    def wait_near(src, dst, send, recv):
        @pl.when(has_left)
        def _():
            near_left(src, dst, rows, send, recv).wait_send()
            near_right(src, dst, rows, send, recv).wait_recv()

        @pl.when(has_right)
        def _():
            near_right(src, dst, rows, send, recv).wait_send()
            near_left(src, dst, rows, send, recv).wait_recv()

    piece = rows // DEG

    def start_piece(k):
        for link in reversed(range(NEXP)):
            far(node_ref, npool_ref, link, nsend, nrecv, pl.multiple_of(k * piece, piece), piece).start()

    for copy in own_copies:
        copy.start()

    for b in range(count):
        wide = jnp.concatenate([ops_ref[b, j] for j in range(NL)], axis=1)
        hi = wide.astype(BF16)
        opcat[b, 0:BS] = hi
        opcat[b, BS : 2 * BS] = (wide - hi.astype(F32)).astype(BF16)

    first = me * count - REACH

    def group(blocks, k, par, factor):
        src, dst, term = pools[1 - par], pools[par], terms[par]
        news = []
        for b in blocks:
            picked = jnp.concatenate(
                [src[jnp.clip(lap_ref[b, j] - first, 0, count + 2 * REACH - 1)] for j in range(NL)], axis=0
            )
            r = jnp.dot(opcat[b], picked, preferred_element_type=F32)
            r = r[:BS] + r[BS:]
            r = r[:, : r.shape[1] // 2] + r[:, r.shape[1] // 2 :]
            news.append(factor * r - term[b])
        sums = [enc[b] + coef_ref[k] * new for b, new in zip(blocks, news)]
        for b, new, total in zip(blocks, news, sums):
            dst[REACH + b] = split(new)
            term[b] = new
            enc[b] = total

    edges = [*range(REACH), *range(count - REACH, count)]
    inner = list(range(REACH, count - REACH))

    def two_steps(i, carry):
        k = 2 * i + 1
        wait_halo(k - 1, 0)

        @pl.when(i > 0)
        def _():
            wait_halo_sent(k - 2, 1)

        factor = jnp.where(i == 0, 1.0, 2.0).astype(F32)
        group(edges, k, 1, factor)
        start_halo(k, 1)
        start_piece(k - 1)
        group(inner, k, 1, factor)
        k = 2 * i + 2
        wait_halo(k - 1, 1)
        wait_halo_sent(k - 2, 0)
        group(edges, k, 0, 2.0)

        @pl.when(k < DEG)
        def _():
            start_halo(k, 0)

        start_piece(k - 1)
        group(inner, k, 0, 2.0)
        return carry

    lax.fori_loop(0, DEG // 2, two_steps, 0)
    wait_halo_sent(DEG - 1, 1)

    epool_ref[pl.ds(rim, rows)] = enc[...].reshape(rows, -1).astype(BF16)
    own_enc = epool_ref.at[pl.ds(rim, rows)]
    start_near(own_enc, epool_ref, esend, erecv)
    for link in range(NEXP):
        far(own_enc, epool_ref, link, esend, erecv).start()
    start_near(node_ref, npool_ref, nsend, nrecv)
    for copy in own_copies:
        copy.wait()

    tile = 512

    def blend(at, size):
        x = jnp.dot(epool_ref[at], we_ref[...], preferred_element_type=F32)
        blended[0:size] = (npool_ref[at].astype(F32) + x).astype(BF16)

    def keys_values(row, size):
        def columns(t, carry):
            cols = pl.ds(pl.multiple_of(D + t * tile, tile), tile)
            y = jnp.dot(blended[0:size], wqkv_ref[:, cols], preferred_element_type=F32).astype(BF16)
            to = pl.ds(pl.multiple_of(t * tile, tile), tile)
            kv[row // BS : (row + size) // BS, :, to] = y.reshape(size // BS, BS, tile)
            return carry

        lax.fori_loop(0, 2 * D // tile, columns, 0)

    blend(pl.ds(rim, rows), rows)

    def queries(t, carry):
        cols = pl.ds(pl.multiple_of(t * tile, tile), tile)
        y = jnp.dot(blended[0:rows], wqkv_ref[:, cols], preferred_element_type=F32).astype(BF16)
        qs[:, cols] = y * jnp.array(1.0 / HD**0.5, BF16)
        return carry

    lax.fori_loop(0, D // tile, queries, 0)
    keys_values(rim, rows)
    for link in range(NEXP):
        for src, dst, send, recv in ((own_enc, epool_ref, esend, erecv), (node_ref, npool_ref, nsend, nrecv)):
            copy = far(src, dst, link, send, recv)
            copy.wait_send()
            copy.wait_recv()
        row = 2 * rim + rows + link * rows
        blend(pl.ds(row, rows), rows)
        keys_values(row, rows)
        if link == 0:
            wait_near(own_enc, epool_ref, esend, erecv)
            wait_near(node_ref, npool_ref, nsend, nrecv)
            for row in (0, rim + rows):
                blend(pl.ds(row, rim), rim)
                keys_values(row, rim)

    pack = 4
    width = pack * HD
    head = lax.broadcasted_iota(jnp.int32, (BS, width), 1) // HD
    keep = [head == h for h in range(pack)]

    def attend(b, carry):
        at = pl.ds(pl.multiple_of(b * BS, BS), BS)
        where = [slots_ref[b, j] for j in range(1 + NL + NEXP)]
        results = []
        for g in range(HEADS // pack):
            cols = slice(g * width, (g + 1) * width)
            vcols = slice(D + g * width, D + (g + 1) * width)
            q = qs[at, cols]
            q = jnp.concatenate([jnp.where(m, q, jnp.zeros_like(q)) for m in keep], axis=0)
            k = jnp.concatenate([kv[w, :, cols] for w in where], axis=0)
            v = jnp.concatenate([kv[w, :, vcols] for w in where], axis=0)
            s = lax.dot_general(q, k, (((1,), (1,)), ((), ())), preferred_element_type=F32)
            p = jnp.exp(s - jnp.max(s, axis=1, keepdims=True))
            p = (p * (1.0 / jnp.sum(p, axis=1, keepdims=True))).astype(BF16)
            o = jnp.dot(p, v, preferred_element_type=F32)
            mine = o[0:BS]
            for h in range(1, pack):
                mine = jnp.where(keep[h], o[h * BS : (h + 1) * BS], mine)
            results.append(mine.astype(BF16))
        for g, result in enumerate(results):
            att[at, g * width : (g + 1) * width] = result
        return carry

    lax.fori_loop(0, count, attend, 0)

    def output(t, carry):
        cols = pl.ds(pl.multiple_of(t * tile, tile), tile)
        out_ref[:, cols] = jnp.dot(att[...], wo_ref[:, cols], preferred_element_type=F32).astype(BF16)
        return carry

    lax.fori_loop(0, D // tile, output, 0)


def on_device(
    n,
    node_feats,
    struct_feats,
    op_blocks,
    laplace_index,
    graph_links,
    expander_slot,
    series_coef,
    encode_weight,
    qkv_weight,
    out_weight,
):
    count = op_blocks.shape[0]
    rows, rim, pch = count * BS, REACH * BS, struct_feats.shape[1]
    pool_rows = rows * (1 + NEXP) + 2 * rim
    vmem = pl.BlockSpec(memory_space=pltpu.VMEM)
    smem = pl.BlockSpec(memory_space=pltpu.SMEM)
    hbm = pl.BlockSpec(memory_space=pl.ANY)
    dma = pltpu.SemaphoreType.DMA
    first_block = lax.axis_index("seq") * count
    own_slot = jnp.arange(count, dtype=jnp.int32)[:, None] + REACH
    graph_slot = graph_links - first_block + REACH
    far_base = count + 2 * REACH + jnp.arange(NEXP, dtype=jnp.int32) * count
    slots = jnp.concatenate([own_slot, graph_slot, far_base[None, :] + expander_slot], axis=1)
    return pl.pallas_call(
        functools.partial(layer_kernel, n),
        out_shape=jax.ShapeDtypeStruct((rows, D), BF16),
        in_specs=[hbm, vmem, vmem, smem, smem, smem, hbm, hbm, hbm],
        out_specs=vmem,
        scratch_shapes=[
            pltpu.VMEM((count + 2 * REACH, BS, 2 * pch), BF16),
            pltpu.VMEM((count + 2 * REACH, BS, 2 * pch), BF16),
            pltpu.VMEM((DEG, 2, REACH, BS, 2 * pch), BF16),
            pltpu.VMEM((count, BS, pch), F32),
            pltpu.VMEM((count, BS, pch), F32),
            pltpu.VMEM((count, BS, pch), F32),
            pltpu.VMEM((count, 2 * BS, NL * BS), BF16),
            pltpu.VMEM((pool_rows, D), BF16),
            pltpu.VMEM((pool_rows, pch), BF16),
            pltpu.VMEM(encode_weight.shape, BF16),
            pltpu.VMEM(qkv_weight.shape, BF16),
            pltpu.VMEM(out_weight.shape, BF16),
            pltpu.VMEM((rows, D), BF16),
            pltpu.VMEM((pool_rows // BS, BS, 2 * D), BF16),
            pltpu.VMEM((rows, D), BF16),
            pltpu.VMEM((rows, D), BF16),
            dma((DEG, 2)),
            dma((DEG, 2)),
            dma((NEXP + 2,)),
            dma((NEXP + 2,)),
            dma((NEXP + 2,)),
            dma((NEXP + 2,)),
            dma((4,)),
        ],
        compiler_params=pltpu.CompilerParams(
            collective_id=0, has_side_effects=True, vmem_limit_bytes=VMEM_LIMIT
        ),
    )(
        node_feats,
        struct_feats,
        op_blocks,
        laplace_index,
        slots,
        series_coef,
        encode_weight,
        qkv_weight,
        out_weight,
    )


def solution(mesh):
    placed = (
        P(("group", "seq"), None),
        P(("group", "seq"), None),
        P(("group", "seq"), None, None, None),
        P(("group", "seq"), None),
        P(("group", "seq"), None),
        P(("group", "seq"), None),
        P(),
        P(),
        P(),
        P(),
    )
    return jax.shard_map(
        functools.partial(on_device, mesh.shape["seq"]),
        mesh=mesh,
        in_specs=placed,
        out_specs=P(("group", "seq"), None),
        check_vma=False,
    )
```

time: 129 us -> 102 us (0.79); the launches traced: 127 us -> 102 us
  Pallas kernels: 124 us -> 95.9 us
  local copies, waits for them, and re-layouts: 2.86 us -> 5.12 us
    pallas_call x2 -> x1, Pallas kernels: 124 us -> 95.9 us  [on_device(): pl.pallas_call(functools.partial(layer_kernel, n), out_shape=jax.ShapeDty...]
    unnamed x3 -> x4, local copies, waits for them, and re-layouts: 2.86 us -> 5.12 us
where the time goes in v2:
time: 102 us
  Pallas kernels  95.9 us (94%)
  local copies, waits for them, and re-layouts  5.12 us (5%)
    pallas_call x1, Pallas kernels, on_device(): pl.pallas_call(functools.partial(layer_kernel, n), out_shape=jax.ShapeDty...  95.9 us
    unnamed x4, local copies, waits for them, and re-layouts  5.12 us

profile of v2, /device:TPU:3, one launch (start us, length us, event | category | flops | bytes accessed | tf_op | source)
XLA Modules:
  0.0 101.8 jit_solution(16190275112426295940)
XLA Ops:
  0.0 1.3 %copy.13.lap_ref = s32[8,3]{1,0:T(8,128)} copy(s32[8,3]{0,1:T(4,128)} %param.13) | data formatting | bytes 192 | tf_op args[3]
  1.4 0.8 copy.11
  2.1 0.8 copy.12
  2.9 0.7 pad_add_fusion.slots_ref
  3.5 95.9 %shard_map.100 = bf16[512,1024]{1,0:T(8,128)(2,1)} custom-call(bf16[512,1024]{1,0:T(8,128)(2,1)} %node_ref.1, f32[512,128]{1,0:T(8,128)} %struct_ref.1, f32[8,3,64,64]{3,2,1,0:T(8,128)} %ops_ref.1, s32[8,3]{1,0:T(8,128)} %copy.13.lap_ref, s32[8,8]{1,0:T(8,128)} %pad_add_fusion.slots_ref, f32[9]{0:T(128)} %coef_ref.1, bf16[128,1024]{1,0:T(8,128)(2,1)} %we_hbm.1, ...), custom_call_target="tpu_custom_call" | custom-call | tf_op jit(solution)/shard_map/pallas_call | solution.py:369
  99.5 2.3 %copy.15 = bf16[512,1024]{1,0:T(8,128)(2,1)} copy(bf16[512,1024]{1,0:T(8,128)(2,1)} %shard_map.100) | data formatting | bytes 2097152
  (4 shorter events, 0.0 us)

commit v3 on v2

--- a/solution.py
+++ b/solution.py
@@ -187,12 +187,22 @@
             near_right(src, dst, rows, send, recv).wait_send()
             near_left(src, dst, rows, send, recv).wait_recv()
 
-    piece = rows // DEG
+    sizes = [rows // DEG if link < NEXP // 2 else rows // DEG * 3 // 4 for link in range(NEXP)]
 
     def start_piece(k):
         for link in reversed(range(NEXP)):
-            far(node_ref, npool_ref, link, nsend, nrecv, pl.multiple_of(k * piece, piece), piece).start()
-
+            at = k * sizes[link]
+            if not isinstance(k, int):
+                at = pl.multiple_of(at, 16)
+            far(node_ref, npool_ref, link, nsend, nrecv, at, sizes[link]).start()
+
+    def start_rest():
+        for link in range(NEXP):
+            sent = DEG * sizes[link]
+            if sent < rows:
+                far(node_ref, npool_ref, link, nsend, nrecv, sent, rows - sent).start()
+
+    start_piece(0)
     for copy in own_copies:
         copy.start()
 
@@ -235,7 +245,7 @@
         factor = jnp.where(i == 0, 1.0, 2.0).astype(F32)
         group(edges, k, 1, factor)
         start_halo(k, 1)
-        start_piece(k - 1)
+        start_piece(k)
         group(inner, k, 1, factor)
         k = 2 * i + 2
         wait_halo(k - 1, 1)
@@ -245,8 +255,8 @@
         @pl.when(k < DEG)
         def _():
             start_halo(k, 0)
-
-        start_piece(k - 1)
+            start_piece(k)
+
         group(inner, k, 0, 2.0)
         return carry
 
@@ -259,6 +269,7 @@
     for link in range(NEXP):
         far(own_enc, epool_ref, link, esend, erecv).start()
     start_near(node_ref, npool_ref, nsend, nrecv)
+    start_rest()
     for copy in own_copies:
         copy.wait()
 

time: 102 us -> 94.4 us (0.925)
  Pallas kernels: 95.9 us -> 88.3 us
    pallas_call x1, Pallas kernels: 95.9 us -> 88.3 us  [on_device(): pl.pallas_call(functools.partial(layer_kernel, n), out_shape=jax.ShapeDty...]
where the time goes in v3:
time: 94.4 us; the launch traced here: 94.1 us
  Pallas kernels  88.3 us (94%)
  local copies, waits for them, and re-layouts  5.12 us (5%)
    pallas_call x1, Pallas kernels, on_device(): pl.pallas_call(functools.partial(layer_kernel, n), out_shape=jax.ShapeDty...  88.3 us
    unnamed x4, local copies, waits for them, and re-layouts  5.12 us

profile of v3, /device:TPU:3, one launch (start us, length us, event | category | flops | bytes accessed | tf_op | source)
XLA Modules:
  0.0 94.1 jit_solution(13990993637022461544)
XLA Ops:
  0.0 1.3 %copy.13.lap_ref = s32[8,3]{1,0:T(8,128)} copy(s32[8,3]{0,1:T(4,128)} %param.13) | data formatting | bytes 192 | tf_op args[3]
  1.4 0.8 copy.11
  2.1 0.8 copy.12
  2.9 0.7 pad_add_fusion.slots_ref
  3.5 88.3 %shard_map.100 = bf16[512,1024]{1,0:T(8,128)(2,1)} custom-call(bf16[512,1024]{1,0:T(8,128)(2,1)} %node_ref.1, f32[512,128]{1,0:T(8,128)} %struct_ref.1, f32[8,3,64,64]{3,2,1,0:T(8,128)} %ops_ref.1, s32[8,3]{1,0:T(8,128)} %copy.13.lap_ref, s32[8,8]{1,0:T(8,128)} %pad_add_fusion.slots_ref, f32[9]{0:T(128)} %coef_ref.1, bf16[128,1024]{1,0:T(8,128)(2,1)} %we_hbm.1, ...), custom_call_target="tpu_custom_call" | custom-call | tf_op jit(solution)/shard_map/pallas_call | solution.py:380
  91.9 2.3 %copy.15 = bf16[512,1024]{1,0:T(8,128)(2,1)} copy(bf16[512,1024]{1,0:T(8,128)(2,1)} %shard_map.100) | data formatting | bytes 2097152
  (4 shorter events, 0.0 us)

commit v4 on v3

--- a/solution.py
+++ b/solution.py
@@ -187,7 +187,7 @@
             near_right(src, dst, rows, send, recv).wait_send()
             near_left(src, dst, rows, send, recv).wait_recv()
 
-    sizes = [rows // DEG if link < NEXP // 2 else rows // DEG * 3 // 4 for link in range(NEXP)]
+    sizes = [rows // DEG if link < NEXP // 2 else rows // DEG // 2 for link in range(NEXP)]
 
     def start_piece(k):
         for link in reversed(range(NEXP)):

time: 94.4 us -> 98.6 us (1.044); the launches traced: 94.1 us -> 97 us
  Pallas kernels: 88.3 us -> 91.2 us
    pallas_call x1, Pallas kernels: 88.3 us -> 91.2 us  [on_device(): pl.pallas_call(functools.partial(layer_kernel, n), out_shape=jax.ShapeDty...]
where the time goes in v4:
time: 98.6 us; the launch traced here: 97 us
  Pallas kernels  91.2 us (92%)
  local copies, waits for them, and re-layouts  5.12 us (5%)
    pallas_call x1, Pallas kernels, on_device(): pl.pallas_call(functools.partial(layer_kernel, n), out_shape=jax.ShapeDty...  91.2 us
    unnamed x4, local copies, waits for them, and re-layouts  5.12 us

profile of v4, /device:TPU:3, one launch (start us, length us, event | category | flops | bytes accessed | tf_op | source)
XLA Modules:
  0.0 97.0 jit_solution(4808386469050709940)
XLA Ops:
  0.0 1.3 %copy.13.lap_ref = s32[8,3]{1,0:T(8,128)} copy(s32[8,3]{0,1:T(4,128)} %param.13) | data formatting | bytes 192 | tf_op args[3]
  1.4 0.8 copy.11
  2.1 0.8 copy.12
  2.9 0.7 pad_add_fusion.slots_ref
  3.5 91.2 %shard_map.100 = bf16[512,1024]{1,0:T(8,128)(2,1)} custom-call(bf16[512,1024]{1,0:T(8,128)(2,1)} %node_ref.1, f32[512,128]{1,0:T(8,128)} %struct_ref.1, f32[8,3,64,64]{3,2,1,0:T(8,128)} %ops_ref.1, s32[8,3]{1,0:T(8,128)} %copy.13.lap_ref, s32[8,8]{1,0:T(8,128)} %pad_add_fusion.slots_ref, f32[9]{0:T(128)} %coef_ref.1, bf16[128,1024]{1,0:T(8,128)(2,1)} %we_hbm.1, ...), custom_call_target="tpu_custom_call" | custom-call | tf_op jit(solution)/shard_map/pallas_call | solution.py:380
  94.7 2.3 %copy.15 = bf16[512,1024]{1,0:T(8,128)(2,1)} copy(bf16[512,1024]{1,0:T(8,128)(2,1)} %shard_map.100) | data formatting | bytes 2097152
  (4 shorter events, 0.0 us)
